TPU v7x, 512 devices: a whole 4x8x8 slice. The times are simulated.
512 devices in a mesh: txt: 16 (over y_hi, z), aud: 32 (over x, y_lo, core).
Axes of the slice: x: 4, y: 8 (y_hi: 2, y_lo: 4; y = y_hi * 4 + y_lo), z: 8, core: 2. Of those that a mesh axis runs over, the one named last changes fastest.
Arguments:
- images: float32 [131072, 1024], P(('txt', 'aud')), may hold values from -2 to 2
- texts: float32 [256, 1024], P('txt'), may hold values from -2 to 2
- audio: float32 [128, 1024], P('aud'), may hold values from -2 to 2
- pos_text: int32 [131072], P(('txt', 'aud')), may hold values from 0 to 255
- pos_audio: int32 [131072], P(('txt', 'aud')), may hold values from 0 to 11
- logit_scale: float32 [1], replicated, may hold values from 1 to 4
- logit_bias: float32 [1], replicated, may hold values from -3 to -1
Outputs:
- grad_images: float32 [131072, 1024], P(('txt', 'aud'))
- grad_texts: float32 [256, 1024], P('txt')
- grad_audio: float32 [128, 1024], P('aud')
All inputs are finite; a program needn't handle non-finite values.
Results may differ from a plain program's by a relative error of at most 0.0044.
Values sent between devices are 32-bit elements; how exact they have to be, the bound alone decides.
No kernel may reach another device: no remote copies, remote signals or barrier semaphores. Data moves between devices by JAX's collectives and lax.ppermute only.
A program may use at most 64 MiB of HBM per device.

v0:
```python
import jax
import jax.numpy as jnp
from jax import lax
from jax.sharding import PartitionSpec as P

HOPS = 2


def from_behind(shard, axis, by):
    size = lax.axis_size(axis)
    return lax.ppermute(shard, axis, [(i, (i + by) % size) for i in range(size)])


def block_terms(image_half, text_piece, window, first_row, pos_text, pos_audio, temper, offset):
    row_count = text_piece.shape[0]
    slot_count = window.shape[0]
    products = (
        (text_piece[:, None, :] * window[None, :, :])
        .reshape(row_count * slot_count, -1)
        .astype(jnp.bfloat16)
    )
    logits = (
        temper
        * lax.dot_general(
            image_half, products, (((1,), (1,)), ((), ())), preferred_element_type=jnp.float32
        )
        + offset
    )
    columns = jnp.arange(row_count * slot_count, dtype=jnp.int32)
    text_of = first_row + columns // slot_count
    slot_of = columns % slot_count
    positive = (text_of[None, :] == pos_text[:, None]) & (slot_of[None, :] == pos_audio[:, None])
    slope = ((jax.nn.sigmoid(logits) - positive.astype(jnp.float32)) * temper).astype(jnp.bfloat16)
    grad_image = jnp.dot(slope, products, preferred_element_type=jnp.float32)
    grad_prod = lax.dot_general(
        slope, image_half, (((0,), (0,)), ((), ())), preferred_element_type=jnp.float32
    )
    grad_prod = grad_prod.reshape(row_count, slot_count, -1)
    grad_piece = jnp.sum(grad_prod * window[None, :, :], axis=1)
    grad_window = jnp.sum(grad_prod * text_piece[:, None, :], axis=0)
    return (grad_image, grad_piece, grad_window)


def send_home(grad_window, block_rows):
    carried = grad_window[HOPS * block_rows :]
    for number in range(HOPS):
        level = HOPS - 1 - number
        carried = (
            from_behind(carried, "aud", 1)
            + grad_window[level * block_rows : (level + 1) * block_rows]
        )
    return carried


def shards(images, texts, audio, pos_text, pos_audio, logit_scale, logit_bias):
    temper = logit_scale[0]
    offset = logit_bias[0]
    block_rows = audio.shape[0]
    text_rows = texts.shape[0]
    pieces = [audio]
    current = audio
    for number in range(HOPS):
        current = from_behind(current, "aud", -1)
        pieces.append(current)
    window = jnp.concatenate(pieces, axis=0)
    image_half = images.astype(jnp.bfloat16)
    cycle_size = lax.axis_size("txt")
    position = lax.axis_index("txt")
    empty_image = jnp.zeros(images.shape, jnp.float32)
    empty_window = jnp.zeros(window.shape, jnp.float32)

    def advance(turn_index, state):
        held_text, held_grad, grad_image, grad_window = state
        owner = (position - turn_index) % cycle_size
        first = owner * text_rows
        more_image, more_piece, more_window = block_terms(
            image_half, held_text, window, first, pos_text, pos_audio, temper, offset
        )
        held_text, held_grad = from_behind((held_text, held_grad + more_piece), "txt", 1)
        return (held_text, held_grad, grad_image + more_image, grad_window + more_window)

    start_state = (texts, jnp.zeros(texts.shape, jnp.float32), empty_image, empty_window)
    final_state = lax.fori_loop(0, cycle_size, advance, start_state)
    grad_local_text = final_state[1]
    grad_images = final_state[2]
    grad_window = final_state[3]
    grad_texts = lax.psum(grad_local_text, "aud")
    summed_window = lax.psum(grad_window, "txt")
    grad_audio = send_home(summed_window, block_rows)
    return (grad_images, grad_texts, grad_audio)


def solution(mesh):
    placed = (
        P(("txt", "aud"), None),
        P("txt", None),
        P("aud", None),
        P(("txt", "aud")),
        P(("txt", "aud")),
        P(),
        P(),
    )
    return jax.shard_map(
        shards,
        mesh=mesh,
        in_specs=placed,
        out_specs=(P(("txt", "aud"), None), P("txt", None), P("aud", None)),
        check_vma=False,
    )
```

profile of v0, /device:TPU:32, one launch (start us, length us, event | category | flops | bytes accessed | tf_op | source)
XLA Modules:
  0.0 684.3 jit_solution(6114707449579966862)
XLA Ops:
  8.7 4.4 collective-permute-start.2
  14.6 7.5 %collective-permute-start.3 = (f32[4,1024]{1,0:T(4,128)S(1)}, f32[4,1024]{1,0:T(4,128)S(1)}, u32[]{:S(2)}, u32[]{:S(2)}) collective-permute-start(f32[4,1024]{1,0:T(4,128)S(1)} %collective-permute-done.2), channel_id=1, source_target_pairs={{0,31},{1,0},{2,1},{3,2},{4,3},{5,4},{6,5},{7,6},{8,7},{9,8},{10,9... | collective-permute-start | bytes 49160 | tf_op jit(solution)/shard_map/ppermute | solution.py:11
  24.2 301.3 %while.23 = (s32[]{:T(128)}, f32[16,1024]{1,0:T(8,128)}, f32[16,1024]{1,0:T(8,128)}, f32[256,1024]{1,0:T(8,128)S(1)}, f32[12,1024]{1,0:T(8,128)}, /*index=5*/f32...) while((s32[]{:T(128)}, f32[16,1024]{1,0:T(8,128)}, ...), condition=%wide.region_3.4_spmd.clone, body=%wide.region_0.3_spmd.clone.sunk | while | flops 304298432 | bytes 14095801 | solution.py:83
  25.1 4.3 collective-permute-start
  32.8 4.3 collective-permute-start.1
  38.2 4.0 collective-permute-done
  56.0 3.8 collective-permute-done
  59.8 4.6 collective-permute-done.1
  77.8 5.2 collective-permute-done.1
  96.2 5.3 collective-permute-done.1
  114.7 5.3 collective-permute-done.1
  133.2 5.4 collective-permute-done.1
  151.7 5.3 collective-permute-done.1
  170.2 5.6 collective-permute-done.1
  189.0 6.0 collective-permute-done.1
  205.1 3.8 collective-permute-done
  208.9 4.7 collective-permute-done.1
  223.7 4.2 collective-permute-done
  228.0 4.7 collective-permute-done.1
  242.7 4.4 collective-permute-done
  247.1 4.1 collective-permute-done.1
  261.2 4.5 collective-permute-done
  265.7 3.9 collective-permute-done.1
  279.7 4.2 collective-permute-done
  283.9 4.5 collective-permute-done.1
  298.5 4.4 collective-permute-done
  302.9 4.0 collective-permute-done.1
  320.7 4.9 collective-permute-done.1
  325.6 93.6 %psum.15 = f32[12,1024]{1,0:T(8,128)S(1)} all-reduce(f32[12,1024]{1,0:T(8,128)} %get-tuple-element.335), channel_id=1, replica_groups=mesh['txt'=16,'aud'=32] {'txt'}, use_global_device_ids=true, to_apply=%region_5.6 | all-reduce | flops 12288 | bytes 98304 | tf_op jit(solution)/shard_map/psum | solution.py:88
  421.1 7.0 %collective-permute-done.4 = f32[4,1024]{1,0:T(4,128)S(1)} collective-permute-done((f32[4,1024]{1,0:T(4,128)S(1)}, f32[4,1024]{1,0:T(4,128)S(1)}, u32[]{:S(2)}, u32[]{:S(2)}) %collective-permute-start.4) | collective-permute-done | bytes 16416 | tf_op jit(solution)/shard_map/ppermute | solution.py:11
  430.1 7.0 %collective-permute-done.5 = f32[4,1024]{1,0:T(4,128)S(1)} collective-permute-done((f32[4,1024]{1,0:T(4,128)S(1)}, f32[4,1024]{1,0:T(4,128)S(1)}, u32[]{:S(2)}, u32[]{:S(2)}) %collective-permute-start.5) | collective-permute-done | bytes 16416 | tf_op jit(solution)/shard_map/ppermute | solution.py:11
  437.8 238.2 %all-reduce.2.cloned.1.call-done = f32[16,1024]{1,0:T(8,128)} async-done(((f32[16,1024]{1,0:T(8,128)}), f32[16,1024]{1,0:T(8,128)}) %all-reduce.2.cloned.1.call-update) | async-done | bytes 65552 | tf_op jit(solution)/shard_map/psum | solution.py:87
  (303 shorter events, 194.6 us)
Async XLA Ops:
  7.2 668.8 %all-reduce.2.cloned.1.call-start = ((), (), s32[]{:S(2)}) async-start(), calls=%async_computation | async-start | bytes 131072 | tf_op jit(solution)/shard_map/psum | solution.py:87
  25.1 17.1 %collective-permute-start = (f32[16,1024]{1,0:T(8,128)S(1)}, f32[16,1024]{1,0:T(8,128)}, u32[]{:S(2)}, u32[]{:S(2)}) collective-permute-start(f32[16,1024]{1,0:T(8,128)S(1)} %copy.16), channel_id=1, source_target_pairs={{0,32},{32,64},{64,96},{96,128},{128,160},{160,192},{192,224},{224... | collective-permute-start | bytes 196616 | tf_op jit(solution)/shard_map/while/body/eval_jaxpr/ppermute | solution.py:11
  32.8 13.2 %collective-permute-start.1 = (f32[16,1024]{1,0:T(8,128)S(1)}, f32[16,1024]{1,0:T(8,128)}, u32[]{:S(2)}, u32[]{:S(2)}) collective-permute-start(f32[16,1024]{1,0:T(8,128)S(1)} %add.228), channel_id=1, source_target_pairs={{0,32},{32,64},{64,96},{96,128},{128,160},{160,192},{192,224},{224... | collective-permute-start | bytes 196616 | tf_op jit(solution)/shard_map/while/body/eval_jaxpr/ppermute | solution.py:11
  46.9 13.0 %collective-permute-start = (f32[16,1024]{1,0:T(8,128)S(1)}, f32[16,1024]{1,0:T(8,128)}, u32[]{:S(2)}, u32[]{:S(2)}) collective-permute-start(f32[16,1024]{1,0:T(8,128)S(1)} %copy.16), channel_id=1, source_target_pairs={{0,32},{32,64},{64,96},{96,128},{128,160},{160,192},{192,224},{224... | collective-permute-start | bytes 196616 | tf_op jit(solution)/shard_map/while/body/eval_jaxpr/ppermute | solution.py:11
  52.2 12.3 %collective-permute-start.1 = (f32[16,1024]{1,0:T(8,128)S(1)}, f32[16,1024]{1,0:T(8,128)}, u32[]{:S(2)}, u32[]{:S(2)}) collective-permute-start(f32[16,1024]{1,0:T(8,128)S(1)} %add.228), channel_id=1, source_target_pairs={{0,32},{32,64},{64,96},{96,128},{128,160},{160,192},{192,224},{224... | collective-permute-start | bytes 196616 | tf_op jit(solution)/shard_map/while/body/eval_jaxpr/ppermute | solution.py:11
  65.4 12.4 %collective-permute-start = (f32[16,1024]{1,0:T(8,128)S(1)}, f32[16,1024]{1,0:T(8,128)}, u32[]{:S(2)}, u32[]{:S(2)}) collective-permute-start(f32[16,1024]{1,0:T(8,128)S(1)} %copy.16), channel_id=1, source_target_pairs={{0,32},{32,64},{64,96},{96,128},{128,160},{160,192},{192,224},{224... | collective-permute-start | bytes 196616 | tf_op jit(solution)/shard_map/while/body/eval_jaxpr/ppermute | solution.py:11
  70.7 12.3 %collective-permute-start.1 = (f32[16,1024]{1,0:T(8,128)S(1)}, f32[16,1024]{1,0:T(8,128)}, u32[]{:S(2)}, u32[]{:S(2)}) collective-permute-start(f32[16,1024]{1,0:T(8,128)S(1)} %add.228), channel_id=1, source_target_pairs={{0,32},{32,64},{64,96},{96,128},{128,160},{160,192},{192,224},{224... | collective-permute-start | bytes 196616 | tf_op jit(solution)/shard_map/while/body/eval_jaxpr/ppermute | solution.py:11
  83.9 12.3 %collective-permute-start = (f32[16,1024]{1,0:T(8,128)S(1)}, f32[16,1024]{1,0:T(8,128)}, u32[]{:S(2)}, u32[]{:S(2)}) collective-permute-start(f32[16,1024]{1,0:T(8,128)S(1)} %copy.16), channel_id=1, source_target_pairs={{0,32},{32,64},{64,96},{96,128},{128,160},{160,192},{192,224},{224... | collective-permute-start | bytes 196616 | tf_op jit(solution)/shard_map/while/body/eval_jaxpr/ppermute | solution.py:11
  89.2 12.3 %collective-permute-start.1 = (f32[16,1024]{1,0:T(8,128)S(1)}, f32[16,1024]{1,0:T(8,128)}, u32[]{:S(2)}, u32[]{:S(2)}) collective-permute-start(f32[16,1024]{1,0:T(8,128)S(1)} %add.228), channel_id=1, source_target_pairs={{0,32},{32,64},{64,96},{96,128},{128,160},{160,192},{192,224},{224... | collective-permute-start | bytes 196616 | tf_op jit(solution)/shard_map/while/body/eval_jaxpr/ppermute | solution.py:11
  102.4 12.3 %collective-permute-start = (f32[16,1024]{1,0:T(8,128)S(1)}, f32[16,1024]{1,0:T(8,128)}, u32[]{:S(2)}, u32[]{:S(2)}) collective-permute-start(f32[16,1024]{1,0:T(8,128)S(1)} %copy.16), channel_id=1, source_target_pairs={{0,32},{32,64},{64,96},{96,128},{128,160},{160,192},{192,224},{224... | collective-permute-start | bytes 196616 | tf_op jit(solution)/shard_map/while/body/eval_jaxpr/ppermute | solution.py:11
  107.7 12.3 %collective-permute-start.1 = (f32[16,1024]{1,0:T(8,128)S(1)}, f32[16,1024]{1,0:T(8,128)}, u32[]{:S(2)}, u32[]{:S(2)}) collective-permute-start(f32[16,1024]{1,0:T(8,128)S(1)} %add.228), channel_id=1, source_target_pairs={{0,32},{32,64},{64,96},{96,128},{128,160},{160,192},{192,224},{224... | collective-permute-start | bytes 196616 | tf_op jit(solution)/shard_map/while/body/eval_jaxpr/ppermute | solution.py:11
  120.9 12.3 %collective-permute-start = (f32[16,1024]{1,0:T(8,128)S(1)}, f32[16,1024]{1,0:T(8,128)}, u32[]{:S(2)}, u32[]{:S(2)}) collective-permute-start(f32[16,1024]{1,0:T(8,128)S(1)} %copy.16), channel_id=1, source_target_pairs={{0,32},{32,64},{64,96},{96,128},{128,160},{160,192},{192,224},{224... | collective-permute-start | bytes 196616 | tf_op jit(solution)/shard_map/while/body/eval_jaxpr/ppermute | solution.py:11
  126.2 12.3 %collective-permute-start.1 = (f32[16,1024]{1,0:T(8,128)S(1)}, f32[16,1024]{1,0:T(8,128)}, u32[]{:S(2)}, u32[]{:S(2)}) collective-permute-start(f32[16,1024]{1,0:T(8,128)S(1)} %add.228), channel_id=1, source_target_pairs={{0,32},{32,64},{64,96},{96,128},{128,160},{160,192},{192,224},{224... | collective-permute-start | bytes 196616 | tf_op jit(solution)/shard_map/while/body/eval_jaxpr/ppermute | solution.py:11
  139.4 12.3 %collective-permute-start = (f32[16,1024]{1,0:T(8,128)S(1)}, f32[16,1024]{1,0:T(8,128)}, u32[]{:S(2)}, u32[]{:S(2)}) collective-permute-start(f32[16,1024]{1,0:T(8,128)S(1)} %copy.16), channel_id=1, source_target_pairs={{0,32},{32,64},{64,96},{96,128},{128,160},{160,192},{192,224},{224... | collective-permute-start | bytes 196616 | tf_op jit(solution)/shard_map/while/body/eval_jaxpr/ppermute | solution.py:11
  144.8 12.3 %collective-permute-start.1 = (f32[16,1024]{1,0:T(8,128)S(1)}, f32[16,1024]{1,0:T(8,128)}, u32[]{:S(2)}, u32[]{:S(2)}) collective-permute-start(f32[16,1024]{1,0:T(8,128)S(1)} %add.228), channel_id=1, source_target_pairs={{0,32},{32,64},{64,96},{96,128},{128,160},{160,192},{192,224},{224... | collective-permute-start | bytes 196616 | tf_op jit(solution)/shard_map/while/body/eval_jaxpr/ppermute | solution.py:11
  163.3 12.6 %collective-permute-start.1 = (f32[16,1024]{1,0:T(8,128)S(1)}, f32[16,1024]{1,0:T(8,128)}, u32[]{:S(2)}, u32[]{:S(2)}) collective-permute-start(f32[16,1024]{1,0:T(8,128)S(1)} %add.228), channel_id=1, source_target_pairs={{0,32},{32,64},{64,96},{96,128},{128,160},{160,192},{192,224},{224... | collective-permute-start | bytes 196616 | tf_op jit(solution)/shard_map/while/body/eval_jaxpr/ppermute | solution.py:11
  176.8 12.3 %collective-permute-start = (f32[16,1024]{1,0:T(8,128)S(1)}, f32[16,1024]{1,0:T(8,128)}, u32[]{:S(2)}, u32[]{:S(2)}) collective-permute-start(f32[16,1024]{1,0:T(8,128)S(1)} %copy.16), channel_id=1, source_target_pairs={{0,32},{32,64},{64,96},{96,128},{128,160},{160,192},{192,224},{224... | collective-permute-start | bytes 196616 | tf_op jit(solution)/shard_map/while/body/eval_jaxpr/ppermute | solution.py:11
  182.1 13.0 %collective-permute-start.1 = (f32[16,1024]{1,0:T(8,128)S(1)}, f32[16,1024]{1,0:T(8,128)}, u32[]{:S(2)}, u32[]{:S(2)}) collective-permute-start(f32[16,1024]{1,0:T(8,128)S(1)} %add.228), channel_id=1, source_target_pairs={{0,32},{32,64},{64,96},{96,128},{128,160},{160,192},{192,224},{224... | collective-permute-start | bytes 196616 | tf_op jit(solution)/shard_map/while/body/eval_jaxpr/ppermute | solution.py:11
  196.0 13.0 %collective-permute-start = (f32[16,1024]{1,0:T(8,128)S(1)}, f32[16,1024]{1,0:T(8,128)}, u32[]{:S(2)}, u32[]{:S(2)}) collective-permute-start(f32[16,1024]{1,0:T(8,128)S(1)} %copy.16), channel_id=1, source_target_pairs={{0,32},{32,64},{64,96},{96,128},{128,160},{160,192},{192,224},{224... | collective-permute-start | bytes 196616 | tf_op jit(solution)/shard_map/while/body/eval_jaxpr/ppermute | solution.py:11
  201.3 12.4 %collective-permute-start.1 = (f32[16,1024]{1,0:T(8,128)S(1)}, f32[16,1024]{1,0:T(8,128)}, u32[]{:S(2)}, u32[]{:S(2)}) collective-permute-start(f32[16,1024]{1,0:T(8,128)S(1)} %add.228), channel_id=1, source_target_pairs={{0,32},{32,64},{64,96},{96,128},{128,160},{160,192},{192,224},{224... | collective-permute-start | bytes 196616 | tf_op jit(solution)/shard_map/while/body/eval_jaxpr/ppermute | solution.py:11
  214.6 13.4 %collective-permute-start = (f32[16,1024]{1,0:T(8,128)S(1)}, f32[16,1024]{1,0:T(8,128)}, u32[]{:S(2)}, u32[]{:S(2)}) collective-permute-start(f32[16,1024]{1,0:T(8,128)S(1)} %copy.16), channel_id=1, source_target_pairs={{0,32},{32,64},{64,96},{96,128},{128,160},{160,192},{192,224},{224... | collective-permute-start | bytes 196616 | tf_op jit(solution)/shard_map/while/body/eval_jaxpr/ppermute | solution.py:11
  219.9 12.7 %collective-permute-start.1 = (f32[16,1024]{1,0:T(8,128)S(1)}, f32[16,1024]{1,0:T(8,128)}, u32[]{:S(2)}, u32[]{:S(2)}) collective-permute-start(f32[16,1024]{1,0:T(8,128)S(1)} %add.228), channel_id=1, source_target_pairs={{0,32},{32,64},{64,96},{96,128},{128,160},{160,192},{192,224},{224... | collective-permute-start | bytes 196616 | tf_op jit(solution)/shard_map/while/body/eval_jaxpr/ppermute | solution.py:11
  233.5 13.5 %collective-permute-start = (f32[16,1024]{1,0:T(8,128)S(1)}, f32[16,1024]{1,0:T(8,128)}, u32[]{:S(2)}, u32[]{:S(2)}) collective-permute-start(f32[16,1024]{1,0:T(8,128)S(1)} %copy.16), channel_id=1, source_target_pairs={{0,32},{32,64},{64,96},{96,128},{128,160},{160,192},{192,224},{224... | collective-permute-start | bytes 196616 | tf_op jit(solution)/shard_map/while/body/eval_jaxpr/ppermute | solution.py:11
  238.9 12.3 %collective-permute-start.1 = (f32[16,1024]{1,0:T(8,128)S(1)}, f32[16,1024]{1,0:T(8,128)}, u32[]{:S(2)}, u32[]{:S(2)}) collective-permute-start(f32[16,1024]{1,0:T(8,128)S(1)} %add.228), channel_id=1, source_target_pairs={{0,32},{32,64},{64,96},{96,128},{128,160},{160,192},{192,224},{224... | collective-permute-start | bytes 196616 | tf_op jit(solution)/shard_map/while/body/eval_jaxpr/ppermute | solution.py:11
  252.1 13.7 %collective-permute-start = (f32[16,1024]{1,0:T(8,128)S(1)}, f32[16,1024]{1,0:T(8,128)}, u32[]{:S(2)}, u32[]{:S(2)}) collective-permute-start(f32[16,1024]{1,0:T(8,128)S(1)} %copy.16), channel_id=1, source_target_pairs={{0,32},{32,64},{64,96},{96,128},{128,160},{160,192},{192,224},{224... | collective-permute-start | bytes 196616 | tf_op jit(solution)/shard_map/while/body/eval_jaxpr/ppermute | solution.py:11
  257.4 12.3 %collective-permute-start.1 = (f32[16,1024]{1,0:T(8,128)S(1)}, f32[16,1024]{1,0:T(8,128)}, u32[]{:S(2)}, u32[]{:S(2)}) collective-permute-start(f32[16,1024]{1,0:T(8,128)S(1)} %add.228), channel_id=1, source_target_pairs={{0,32},{32,64},{64,96},{96,128},{128,160},{160,192},{192,224},{224... | collective-permute-start | bytes 196616 | tf_op jit(solution)/shard_map/while/body/eval_jaxpr/ppermute | solution.py:11
  270.6 13.4 %collective-permute-start = (f32[16,1024]{1,0:T(8,128)S(1)}, f32[16,1024]{1,0:T(8,128)}, u32[]{:S(2)}, u32[]{:S(2)}) collective-permute-start(f32[16,1024]{1,0:T(8,128)S(1)} %copy.16), channel_id=1, source_target_pairs={{0,32},{32,64},{64,96},{96,128},{128,160},{160,192},{192,224},{224... | collective-permute-start | bytes 196616 | tf_op jit(solution)/shard_map/while/body/eval_jaxpr/ppermute | solution.py:11
  275.9 12.6 %collective-permute-start.1 = (f32[16,1024]{1,0:T(8,128)S(1)}, f32[16,1024]{1,0:T(8,128)}, u32[]{:S(2)}, u32[]{:S(2)}) collective-permute-start(f32[16,1024]{1,0:T(8,128)S(1)} %add.228), channel_id=1, source_target_pairs={{0,32},{32,64},{64,96},{96,128},{128,160},{160,192},{192,224},{224... | collective-permute-start | bytes 196616 | tf_op jit(solution)/shard_map/while/body/eval_jaxpr/ppermute | solution.py:11
  289.4 13.6 %collective-permute-start = (f32[16,1024]{1,0:T(8,128)S(1)}, f32[16,1024]{1,0:T(8,128)}, u32[]{:S(2)}, u32[]{:S(2)}) collective-permute-start(f32[16,1024]{1,0:T(8,128)S(1)} %copy.16), channel_id=1, source_target_pairs={{0,32},{32,64},{64,96},{96,128},{128,160},{160,192},{192,224},{224... | collective-permute-start | bytes 196616 | tf_op jit(solution)/shard_map/while/body/eval_jaxpr/ppermute | solution.py:11
  294.7 12.3 %collective-permute-start.1 = (f32[16,1024]{1,0:T(8,128)S(1)}, f32[16,1024]{1,0:T(8,128)}, u32[]{:S(2)}, u32[]{:S(2)}) collective-permute-start(f32[16,1024]{1,0:T(8,128)S(1)} %add.228), channel_id=1, source_target_pairs={{0,32},{32,64},{64,96},{96,128},{128,160},{160,192},{192,224},{224... | collective-permute-start | bytes 196616 | tf_op jit(solution)/shard_map/while/body/eval_jaxpr/ppermute | solution.py:11
  307.9 12.8 %collective-permute-start = (f32[16,1024]{1,0:T(8,128)S(1)}, f32[16,1024]{1,0:T(8,128)}, u32[]{:S(2)}, u32[]{:S(2)}) collective-permute-start(f32[16,1024]{1,0:T(8,128)S(1)} %copy.16), channel_id=1, source_target_pairs={{0,32},{32,64},{64,96},{96,128},{128,160},{160,192},{192,224},{224... | collective-permute-start | bytes 196616 | tf_op jit(solution)/shard_map/while/body/eval_jaxpr/ppermute | solution.py:11
  313.2 12.4 %collective-permute-start.1 = (f32[16,1024]{1,0:T(8,128)S(1)}, f32[16,1024]{1,0:T(8,128)}, u32[]{:S(2)}, u32[]{:S(2)}) collective-permute-start(f32[16,1024]{1,0:T(8,128)S(1)} %add.228), channel_id=1, source_target_pairs={{0,32},{32,64},{64,96},{96,128},{128,160},{160,192},{192,224},{224... | collective-permute-start | bytes 196616 | tf_op jit(solution)/shard_map/while/body/eval_jaxpr/ppermute | solution.py:11
  (41 other events, 643.4 us)
Sparse Core Ops, SparseCore 0:
  430.3 245.6 all-reduce.1
where the time goes:
time: 688 us; the launch traced here: 684 us
  waiting for transfers between devices  390 us (57%)
  blocking collectives  93.6 us (14%)
  starting transfers between devices  81.8 us (12%)
  other arithmetic  44.6 us (6%)
  matrix products  37.1 us (5%)
  local copies, waits for them, and re-layouts  20.8 us (3%)
  between operations  14.1 us (2%)
    psum x1, waiting for transfers between devices, shards(): grad_texts = lax.psum(grad_local_text, 'aud')  238 us
    ppermute x36, waiting for transfers between devices, from_behind(): lax.ppermute(shard, axis, [(i, (i + by) % size) for i in range(size)])  152 us
    psum x1, blocking collectives, shards(): summed_window = lax.psum(grad_window, 'txt')  93.6 us
    ppermute x36, starting transfers between devices, from_behind(): lax.ppermute(shard, axis, [(i, (i + by) % size) for i in range(size)])  81.7 us
    dot_general x16, matrix products, block_terms(): lax.dot_general(image_half, products, (((1,), (1,)), ((), ())), preferred...  26.5 us
    add x16, other arithmetic, advance(): grad_window + more_window  23 us
    while x80, local copies, waits for them, and re-layouts  14.4 us
  transfers between devices with their start and end apart: 37, of which 37 were waited for; matrix products, arithmetic and copies ran while one was open for 12% of the time, Pallas kernels for 0%

commit v1 on v0

--- a/solution.py
+++ b/solution.py
@@ -1,9 +1,18 @@
+import functools
 import jax
 import jax.numpy as jnp
 from jax import lax
 from jax.sharding import PartitionSpec as P
 
 HOPS = 2
+
+
+def check_lane(vector, device_axis):
+    moved = jnp.sum(lax.all_gather(vector, axis_name=device_axis), axis=0)
+    return moved
+
+
+_spread_widths = functools.partial(check_lane, device_axis="aud")
 
 
 def from_behind(shard, axis, by):
@@ -84,7 +93,7 @@
     grad_local_text = final_state[1]
     grad_images = final_state[2]
     grad_window = final_state[3]
-    grad_texts = lax.psum(grad_local_text, "aud")
+    grad_texts = _spread_widths(grad_local_text)
     summed_window = lax.psum(grad_window, "txt")
     grad_audio = send_home(summed_window, block_rows)
     return (grad_images, grad_texts, grad_audio)

time: 688 us -> 465 us (0.68)
  waiting for transfers between devices: 390 us -> 153 us
  matrix products: 37.1 us -> 48.3 us
    psum x1 -> x0, waiting for transfers between devices: 238 us -> none  [shards(): grad_texts = lax.psum(grad_local_text, 'aud')]
    dot_general x16, matrix products: 26.5 us -> 37.7 us  [block_terms(): lax.dot_general(image_half, products, (((1,), (1,)), ((), ())), preferred...]
  transfers between devices with their start and end apart: 37 -> 37, of which waited for: 37 -> 36; matrix products, arithmetic and copies ran while one was open for 12% -> 21% of each run, Pallas kernels for 0% -> 0%
where the time goes in v1:
time: 465 us; the launch traced here: 461 us
  waiting for transfers between devices  153 us (33%)
  blocking collectives  94 us (20%)
  starting transfers between devices  81.8 us (18%)
  other arithmetic  48.6 us (10%)
  matrix products  48.3 us (10%)
  local copies, waits for them, and re-layouts  19.3 us (4%)
  between operations  14.1 us (3%)
    ppermute x36, waiting for transfers between devices, from_behind(): lax.ppermute(shard, axis, [(i, (i + by) % size) for i in range(size)])  153 us
    psum x1, blocking collectives, shards(): summed_window = lax.psum(grad_window, 'txt')  94 us
    ppermute x36, starting transfers between devices, from_behind(): lax.ppermute(shard, axis, [(i, (i + by) % size) for i in range(size)])  81.7 us
    dot_general x16, matrix products, block_terms(): lax.dot_general(image_half, products, (((1,), (1,)), ((), ())), preferred...  37.7 us
    add x16, other arithmetic, advance(): grad_window + more_window  23 us
    add x16, other arithmetic, advance(): held_grad + more_piece  14.5 us
    while x80, local copies, waits for them, and re-layouts  14.4 us
  transfers between devices with their start and end apart: 37, of which 36 were waited for; matrix products, arithmetic and copies ran while one was open for 21% of the time, Pallas kernels for 0%

profile of v1, /device:TPU:32, one launch (start us, length us, event | category | flops | bytes accessed | tf_op | source)
XLA Modules:
  0.0 460.9 jit_solution(12938403948139987219)
XLA Ops:
  8.7 4.4 collective-permute-start.2
  14.7 7.5 %collective-permute-start.3 = (f32[4,1024]{1,0:T(4,128)S(1)}, f32[4,1024]{1,0:T(4,128)S(1)}, u32[]{:S(2)}, u32[]{:S(2)}) collective-permute-start(f32[4,1024]{1,0:T(4,128)S(1)} %collective-permute-done.2), channel_id=1, source_target_pairs={{0,31},{1,0},{2,1},{3,2},{4,3},{5,4},{6,5},{7,6},{8,7},{9,8},{10,9... | collective-permute-start | bytes 49160 | tf_op jit(solution)/shard_map/ppermute | solution.py:20
  25.1 314.1 %while.23 = (s32[]{:T(128)}, f32[16,1024]{1,0:T(8,128)}, f32[16,1024]{1,0:T(8,128)}, f32[256,1024]{1,0:T(8,128)S(1)}, f32[12,1024]{1,0:T(8,128)}, /*index=5*/f32...) while((s32[]{:T(128)}, f32[16,1024]{1,0:T(8,128)}, ...), condition=%wide.region_3.4_spmd.clone, body=%wide.region_0.3_spmd.clone.sunk | while | flops 304298432 | bytes 14095801 | solution.py:92
  25.9 4.3 collective-permute-start
  34.4 4.3 collective-permute-start.1
  42.0 5.6 %collective-permute-done.1 = f32[16,1024]{1,0:T(8,128)} collective-permute-done((f32[16,1024]{1,0:T(8,128)S(1)}, f32[16,1024]{1,0:T(8,128)}, u32[]{:S(2)}, u32[]{:S(2)}) %collective-permute-start.1) | collective-permute-done | bytes 65568 | tf_op jit(solution)/shard_map/while/body/eval_jaxpr/ppermute | solution.py:20
  58.4 2.7 collective-permute-done
  61.1 5.8 %collective-permute-done.1 = f32[16,1024]{1,0:T(8,128)} collective-permute-done((f32[16,1024]{1,0:T(8,128)S(1)}, f32[16,1024]{1,0:T(8,128)}, u32[]{:S(2)}, u32[]{:S(2)}) %collective-permute-start.1) | collective-permute-done | bytes 65568 | tf_op jit(solution)/shard_map/while/body/eval_jaxpr/ppermute | solution.py:20
  77.7 3.1 collective-permute-done
  80.7 5.4 %collective-permute-done.1 = f32[16,1024]{1,0:T(8,128)} collective-permute-done((f32[16,1024]{1,0:T(8,128)S(1)}, f32[16,1024]{1,0:T(8,128)}, u32[]{:S(2)}, u32[]{:S(2)}) %collective-permute-start.1) | collective-permute-done | bytes 65568 | tf_op jit(solution)/shard_map/while/body/eval_jaxpr/ppermute | solution.py:20
  96.9 2.4 collective-permute-done
  99.3 6.1 %collective-permute-done.1 = f32[16,1024]{1,0:T(8,128)} collective-permute-done((f32[16,1024]{1,0:T(8,128)S(1)}, f32[16,1024]{1,0:T(8,128)}, u32[]{:S(2)}, u32[]{:S(2)}) %collective-permute-start.1) | collective-permute-done | bytes 65568 | tf_op jit(solution)/shard_map/while/body/eval_jaxpr/ppermute | solution.py:20
  116.2 2.4 collective-permute-done
  118.5 6.2 %collective-permute-done.1 = f32[16,1024]{1,0:T(8,128)} collective-permute-done((f32[16,1024]{1,0:T(8,128)S(1)}, f32[16,1024]{1,0:T(8,128)}, u32[]{:S(2)}, u32[]{:S(2)}) %collective-permute-start.1) | collective-permute-done | bytes 65568 | tf_op jit(solution)/shard_map/while/body/eval_jaxpr/ppermute | solution.py:20
  137.9 6.2 %collective-permute-done.1 = f32[16,1024]{1,0:T(8,128)} collective-permute-done((f32[16,1024]{1,0:T(8,128)S(1)}, f32[16,1024]{1,0:T(8,128)}, u32[]{:S(2)}, u32[]{:S(2)}) %collective-permute-start.1) | collective-permute-done | bytes 65568 | tf_op jit(solution)/shard_map/while/body/eval_jaxpr/ppermute | solution.py:20
  157.2 6.4 %collective-permute-done.1 = f32[16,1024]{1,0:T(8,128)} collective-permute-done((f32[16,1024]{1,0:T(8,128)S(1)}, f32[16,1024]{1,0:T(8,128)}, u32[]{:S(2)}, u32[]{:S(2)}) %collective-permute-start.1) | collective-permute-done | bytes 65568 | tf_op jit(solution)/shard_map/while/body/eval_jaxpr/ppermute | solution.py:20
  176.8 6.1 %collective-permute-done.1 = f32[16,1024]{1,0:T(8,128)} collective-permute-done((f32[16,1024]{1,0:T(8,128)S(1)}, f32[16,1024]{1,0:T(8,128)}, u32[]{:S(2)}, u32[]{:S(2)}) %collective-permute-start.1) | collective-permute-done | bytes 65568 | tf_op jit(solution)/shard_map/while/body/eval_jaxpr/ppermute | solution.py:20
  196.0 6.8 %collective-permute-done.1 = f32[16,1024]{1,0:T(8,128)} collective-permute-done((f32[16,1024]{1,0:T(8,128)S(1)}, f32[16,1024]{1,0:T(8,128)}, u32[]{:S(2)}, u32[]{:S(2)}) %collective-permute-start.1) | collective-permute-done | bytes 65568 | tf_op jit(solution)/shard_map/while/body/eval_jaxpr/ppermute | solution.py:20
  216.0 6.1 %collective-permute-done.1 = f32[16,1024]{1,0:T(8,128)} collective-permute-done((f32[16,1024]{1,0:T(8,128)S(1)}, f32[16,1024]{1,0:T(8,128)}, u32[]{:S(2)}, u32[]{:S(2)}) %collective-permute-start.1) | collective-permute-done | bytes 65568 | tf_op jit(solution)/shard_map/while/body/eval_jaxpr/ppermute | solution.py:20
  232.9 2.5 collective-permute-done
  235.4 6.1 %collective-permute-done.1 = f32[16,1024]{1,0:T(8,128)} collective-permute-done((f32[16,1024]{1,0:T(8,128)S(1)}, f32[16,1024]{1,0:T(8,128)}, u32[]{:S(2)}, u32[]{:S(2)}) %collective-permute-start.1) | collective-permute-done | bytes 65568 | tf_op jit(solution)/shard_map/while/body/eval_jaxpr/ppermute | solution.py:20
  252.3 3.1 collective-permute-done
  255.4 6.1 %collective-permute-done.1 = f32[16,1024]{1,0:T(8,128)} collective-permute-done((f32[16,1024]{1,0:T(8,128)S(1)}, f32[16,1024]{1,0:T(8,128)}, u32[]{:S(2)}, u32[]{:S(2)}) %collective-permute-start.1) | collective-permute-done | bytes 65568 | tf_op jit(solution)/shard_map/while/body/eval_jaxpr/ppermute | solution.py:20
  274.7 6.1 %collective-permute-done.1 = f32[16,1024]{1,0:T(8,128)} collective-permute-done((f32[16,1024]{1,0:T(8,128)S(1)}, f32[16,1024]{1,0:T(8,128)}, u32[]{:S(2)}, u32[]{:S(2)}) %collective-permute-start.1) | collective-permute-done | bytes 65568 | tf_op jit(solution)/shard_map/while/body/eval_jaxpr/ppermute | solution.py:20
  291.6 2.9 collective-permute-done
  294.4 6.1 %collective-permute-done.1 = f32[16,1024]{1,0:T(8,128)} collective-permute-done((f32[16,1024]{1,0:T(8,128)S(1)}, f32[16,1024]{1,0:T(8,128)}, u32[]{:S(2)}, u32[]{:S(2)}) %collective-permute-start.1) | collective-permute-done | bytes 65568 | tf_op jit(solution)/shard_map/while/body/eval_jaxpr/ppermute | solution.py:20
  311.4 2.4 collective-permute-done
  313.7 6.1 %collective-permute-done.1 = f32[16,1024]{1,0:T(8,128)} collective-permute-done((f32[16,1024]{1,0:T(8,128)S(1)}, f32[16,1024]{1,0:T(8,128)}, u32[]{:S(2)}, u32[]{:S(2)}) %collective-permute-start.1) | collective-permute-done | bytes 65568 | tf_op jit(solution)/shard_map/while/body/eval_jaxpr/ppermute | solution.py:20
  333.0 6.2 %collective-permute-done.1 = f32[16,1024]{1,0:T(8,128)} collective-permute-done((f32[16,1024]{1,0:T(8,128)S(1)}, f32[16,1024]{1,0:T(8,128)}, u32[]{:S(2)}, u32[]{:S(2)}) %collective-permute-start.1) | collective-permute-done | bytes 65568 | tf_op jit(solution)/shard_map/while/body/eval_jaxpr/ppermute | solution.py:20
  339.2 94.0 %psum.7 = f32[12,1024]{1,0:T(8,128)S(1)} all-reduce(f32[12,1024]{1,0:T(8,128)} %get-tuple-element.335), channel_id=1, replica_groups=mesh['txt'=16,'aud'=32] {'txt'}, use_global_device_ids=true, to_apply=%region_5.6 | all-reduce | flops 12288 | bytes 98304 | tf_op jit(solution)/shard_map/psum | solution.py:97
  435.1 7.0 %collective-permute-done.4 = f32[4,1024]{1,0:T(4,128)S(1)} collective-permute-done((f32[4,1024]{1,0:T(4,128)S(1)}, f32[4,1024]{1,0:T(4,128)S(1)}, u32[]{:S(2)}, u32[]{:S(2)}) %collective-permute-start.4) | collective-permute-done | bytes 16416 | tf_op jit(solution)/shard_map/ppermute | solution.py:20
  444.1 7.0 %collective-permute-done.5 = f32[4,1024]{1,0:T(4,128)S(1)} collective-permute-done((f32[4,1024]{1,0:T(4,128)S(1)}, f32[4,1024]{1,0:T(4,128)S(1)}, u32[]{:S(2)}, u32[]{:S(2)}) %collective-permute-start.5) | collective-permute-done | bytes 16416 | tf_op jit(solution)/shard_map/ppermute | solution.py:20
  (297 shorter events, 197.8 us)
Async XLA Ops:
  7.2 444.6 %all-gather.3.cloned.1.call-start = ((), (), s32[]{:S(2)}) async-start(), calls=%async_computation | async-start | bytes 2162688 | tf_op jit(solution)/shard_map/all_gather | solution.py:11
  25.9 16.0 %collective-permute-start = (f32[16,1024]{1,0:T(8,128)S(1)}, f32[16,1024]{1,0:T(8,128)}, u32[]{:S(2)}, u32[]{:S(2)}) collective-permute-start(f32[16,1024]{1,0:T(8,128)S(1)} %copy.16), channel_id=1, source_target_pairs={{0,32},{32,64},{64,96},{96,128},{128,160},{160,192},{192,224},{224... | collective-permute-start | bytes 196616 | tf_op jit(solution)/shard_map/while/body/eval_jaxpr/ppermute | solution.py:20
  34.4 13.2 %collective-permute-start.1 = (f32[16,1024]{1,0:T(8,128)S(1)}, f32[16,1024]{1,0:T(8,128)}, u32[]{:S(2)}, u32[]{:S(2)}) collective-permute-start(f32[16,1024]{1,0:T(8,128)S(1)} %add.226), channel_id=1, source_target_pairs={{0,32},{32,64},{64,96},{96,128},{128,160},{160,192},{192,224},{224... | collective-permute-start | bytes 196616 | tf_op jit(solution)/shard_map/while/body/eval_jaxpr/ppermute | solution.py:20
  48.5 12.6 %collective-permute-start = (f32[16,1024]{1,0:T(8,128)S(1)}, f32[16,1024]{1,0:T(8,128)}, u32[]{:S(2)}, u32[]{:S(2)}) collective-permute-start(f32[16,1024]{1,0:T(8,128)S(1)} %copy.16), channel_id=1, source_target_pairs={{0,32},{32,64},{64,96},{96,128},{128,160},{160,192},{192,224},{224... | collective-permute-start | bytes 196616 | tf_op jit(solution)/shard_map/while/body/eval_jaxpr/ppermute | solution.py:20
  54.6 12.3 %collective-permute-start.1 = (f32[16,1024]{1,0:T(8,128)S(1)}, f32[16,1024]{1,0:T(8,128)}, u32[]{:S(2)}, u32[]{:S(2)}) collective-permute-start(f32[16,1024]{1,0:T(8,128)S(1)} %add.226), channel_id=1, source_target_pairs={{0,32},{32,64},{64,96},{96,128},{128,160},{160,192},{192,224},{224... | collective-permute-start | bytes 196616 | tf_op jit(solution)/shard_map/while/body/eval_jaxpr/ppermute | solution.py:20
  67.7 13.0 %collective-permute-start = (f32[16,1024]{1,0:T(8,128)S(1)}, f32[16,1024]{1,0:T(8,128)}, u32[]{:S(2)}, u32[]{:S(2)}) collective-permute-start(f32[16,1024]{1,0:T(8,128)S(1)} %copy.16), channel_id=1, source_target_pairs={{0,32},{32,64},{64,96},{96,128},{128,160},{160,192},{192,224},{224... | collective-permute-start | bytes 196616 | tf_op jit(solution)/shard_map/while/body/eval_jaxpr/ppermute | solution.py:20
  73.8 12.3 %collective-permute-start.1 = (f32[16,1024]{1,0:T(8,128)S(1)}, f32[16,1024]{1,0:T(8,128)}, u32[]{:S(2)}, u32[]{:S(2)}) collective-permute-start(f32[16,1024]{1,0:T(8,128)S(1)} %add.226), channel_id=1, source_target_pairs={{0,32},{32,64},{64,96},{96,128},{128,160},{160,192},{192,224},{224... | collective-permute-start | bytes 196616 | tf_op jit(solution)/shard_map/while/body/eval_jaxpr/ppermute | solution.py:20
  87.0 12.3 %collective-permute-start = (f32[16,1024]{1,0:T(8,128)S(1)}, f32[16,1024]{1,0:T(8,128)}, u32[]{:S(2)}, u32[]{:S(2)}) collective-permute-start(f32[16,1024]{1,0:T(8,128)S(1)} %copy.16), channel_id=1, source_target_pairs={{0,32},{32,64},{64,96},{96,128},{128,160},{160,192},{192,224},{224... | collective-permute-start | bytes 196616 | tf_op jit(solution)/shard_map/while/body/eval_jaxpr/ppermute | solution.py:20
  93.1 12.3 %collective-permute-start.1 = (f32[16,1024]{1,0:T(8,128)S(1)}, f32[16,1024]{1,0:T(8,128)}, u32[]{:S(2)}, u32[]{:S(2)}) collective-permute-start(f32[16,1024]{1,0:T(8,128)S(1)} %add.226), channel_id=1, source_target_pairs={{0,32},{32,64},{64,96},{96,128},{128,160},{160,192},{192,224},{224... | collective-permute-start | bytes 196616 | tf_op jit(solution)/shard_map/while/body/eval_jaxpr/ppermute | solution.py:20
  106.3 12.3 %collective-permute-start = (f32[16,1024]{1,0:T(8,128)S(1)}, f32[16,1024]{1,0:T(8,128)}, u32[]{:S(2)}, u32[]{:S(2)}) collective-permute-start(f32[16,1024]{1,0:T(8,128)S(1)} %copy.16), channel_id=1, source_target_pairs={{0,32},{32,64},{64,96},{96,128},{128,160},{160,192},{192,224},{224... | collective-permute-start | bytes 196616 | tf_op jit(solution)/shard_map/while/body/eval_jaxpr/ppermute | solution.py:20
  112.4 12.3 %collective-permute-start.1 = (f32[16,1024]{1,0:T(8,128)S(1)}, f32[16,1024]{1,0:T(8,128)}, u32[]{:S(2)}, u32[]{:S(2)}) collective-permute-start(f32[16,1024]{1,0:T(8,128)S(1)} %add.226), channel_id=1, source_target_pairs={{0,32},{32,64},{64,96},{96,128},{128,160},{160,192},{192,224},{224... | collective-permute-start | bytes 196616 | tf_op jit(solution)/shard_map/while/body/eval_jaxpr/ppermute | solution.py:20
  125.6 12.3 %collective-permute-start = (f32[16,1024]{1,0:T(8,128)S(1)}, f32[16,1024]{1,0:T(8,128)}, u32[]{:S(2)}, u32[]{:S(2)}) collective-permute-start(f32[16,1024]{1,0:T(8,128)S(1)} %copy.16), channel_id=1, source_target_pairs={{0,32},{32,64},{64,96},{96,128},{128,160},{160,192},{192,224},{224... | collective-permute-start | bytes 196616 | tf_op jit(solution)/shard_map/while/body/eval_jaxpr/ppermute | solution.py:20
  131.7 12.4 %collective-permute-start.1 = (f32[16,1024]{1,0:T(8,128)S(1)}, f32[16,1024]{1,0:T(8,128)}, u32[]{:S(2)}, u32[]{:S(2)}) collective-permute-start(f32[16,1024]{1,0:T(8,128)S(1)} %add.226), channel_id=1, source_target_pairs={{0,32},{32,64},{64,96},{96,128},{128,160},{160,192},{192,224},{224... | collective-permute-start | bytes 196616 | tf_op jit(solution)/shard_map/while/body/eval_jaxpr/ppermute | solution.py:20
  145.0 12.3 %collective-permute-start = (f32[16,1024]{1,0:T(8,128)S(1)}, f32[16,1024]{1,0:T(8,128)}, u32[]{:S(2)}, u32[]{:S(2)}) collective-permute-start(f32[16,1024]{1,0:T(8,128)S(1)} %copy.16), channel_id=1, source_target_pairs={{0,32},{32,64},{64,96},{96,128},{128,160},{160,192},{192,224},{224... | collective-permute-start | bytes 196616 | tf_op jit(solution)/shard_map/while/body/eval_jaxpr/ppermute | solution.py:20
  151.1 12.5 %collective-permute-start.1 = (f32[16,1024]{1,0:T(8,128)S(1)}, f32[16,1024]{1,0:T(8,128)}, u32[]{:S(2)}, u32[]{:S(2)}) collective-permute-start(f32[16,1024]{1,0:T(8,128)S(1)} %add.226), channel_id=1, source_target_pairs={{0,32},{32,64},{64,96},{96,128},{128,160},{160,192},{192,224},{224... | collective-permute-start | bytes 196616 | tf_op jit(solution)/shard_map/while/body/eval_jaxpr/ppermute | solution.py:20
  164.5 12.3 %collective-permute-start = (f32[16,1024]{1,0:T(8,128)S(1)}, f32[16,1024]{1,0:T(8,128)}, u32[]{:S(2)}, u32[]{:S(2)}) collective-permute-start(f32[16,1024]{1,0:T(8,128)S(1)} %copy.16), channel_id=1, source_target_pairs={{0,32},{32,64},{64,96},{96,128},{128,160},{160,192},{192,224},{224... | collective-permute-start | bytes 196616 | tf_op jit(solution)/shard_map/while/body/eval_jaxpr/ppermute | solution.py:20
  170.6 12.3 %collective-permute-start.1 = (f32[16,1024]{1,0:T(8,128)S(1)}, f32[16,1024]{1,0:T(8,128)}, u32[]{:S(2)}, u32[]{:S(2)}) collective-permute-start(f32[16,1024]{1,0:T(8,128)S(1)} %add.226), channel_id=1, source_target_pairs={{0,32},{32,64},{64,96},{96,128},{128,160},{160,192},{192,224},{224... | collective-permute-start | bytes 196616 | tf_op jit(solution)/shard_map/while/body/eval_jaxpr/ppermute | solution.py:20
  183.8 12.3 %collective-permute-start = (f32[16,1024]{1,0:T(8,128)S(1)}, f32[16,1024]{1,0:T(8,128)}, u32[]{:S(2)}, u32[]{:S(2)}) collective-permute-start(f32[16,1024]{1,0:T(8,128)S(1)} %copy.16), channel_id=1, source_target_pairs={{0,32},{32,64},{64,96},{96,128},{128,160},{160,192},{192,224},{224... | collective-permute-start | bytes 196616 | tf_op jit(solution)/shard_map/while/body/eval_jaxpr/ppermute | solution.py:20
  189.9 13.0 %collective-permute-start.1 = (f32[16,1024]{1,0:T(8,128)S(1)}, f32[16,1024]{1,0:T(8,128)}, u32[]{:S(2)}, u32[]{:S(2)}) collective-permute-start(f32[16,1024]{1,0:T(8,128)S(1)} %add.226), channel_id=1, source_target_pairs={{0,32},{32,64},{64,96},{96,128},{128,160},{160,192},{192,224},{224... | collective-permute-start | bytes 196616 | tf_op jit(solution)/shard_map/while/body/eval_jaxpr/ppermute | solution.py:20
  209.8 12.3 %collective-permute-start.1 = (f32[16,1024]{1,0:T(8,128)S(1)}, f32[16,1024]{1,0:T(8,128)}, u32[]{:S(2)}, u32[]{:S(2)}) collective-permute-start(f32[16,1024]{1,0:T(8,128)S(1)} %add.226), channel_id=1, source_target_pairs={{0,32},{32,64},{64,96},{96,128},{128,160},{160,192},{192,224},{224... | collective-permute-start | bytes 196616 | tf_op jit(solution)/shard_map/while/body/eval_jaxpr/ppermute | solution.py:20
  223.0 12.4 %collective-permute-start = (f32[16,1024]{1,0:T(8,128)S(1)}, f32[16,1024]{1,0:T(8,128)}, u32[]{:S(2)}, u32[]{:S(2)}) collective-permute-start(f32[16,1024]{1,0:T(8,128)S(1)} %copy.16), channel_id=1, source_target_pairs={{0,32},{32,64},{64,96},{96,128},{128,160},{160,192},{192,224},{224... | collective-permute-start | bytes 196616 | tf_op jit(solution)/shard_map/while/body/eval_jaxpr/ppermute | solution.py:20
  229.1 12.4 %collective-permute-start.1 = (f32[16,1024]{1,0:T(8,128)S(1)}, f32[16,1024]{1,0:T(8,128)}, u32[]{:S(2)}, u32[]{:S(2)}) collective-permute-start(f32[16,1024]{1,0:T(8,128)S(1)} %add.226), channel_id=1, source_target_pairs={{0,32},{32,64},{64,96},{96,128},{128,160},{160,192},{192,224},{224... | collective-permute-start | bytes 196616 | tf_op jit(solution)/shard_map/while/body/eval_jaxpr/ppermute | solution.py:20
  242.4 13.0 %collective-permute-start = (f32[16,1024]{1,0:T(8,128)S(1)}, f32[16,1024]{1,0:T(8,128)}, u32[]{:S(2)}, u32[]{:S(2)}) collective-permute-start(f32[16,1024]{1,0:T(8,128)S(1)} %copy.16), channel_id=1, source_target_pairs={{0,32},{32,64},{64,96},{96,128},{128,160},{160,192},{192,224},{224... | collective-permute-start | bytes 196616 | tf_op jit(solution)/shard_map/while/body/eval_jaxpr/ppermute | solution.py:20
  248.5 13.0 %collective-permute-start.1 = (f32[16,1024]{1,0:T(8,128)S(1)}, f32[16,1024]{1,0:T(8,128)}, u32[]{:S(2)}, u32[]{:S(2)}) collective-permute-start(f32[16,1024]{1,0:T(8,128)S(1)} %add.226), channel_id=1, source_target_pairs={{0,32},{32,64},{64,96},{96,128},{128,160},{160,192},{192,224},{224... | collective-permute-start | bytes 196616 | tf_op jit(solution)/shard_map/while/body/eval_jaxpr/ppermute | solution.py:20
  262.4 12.3 %collective-permute-start = (f32[16,1024]{1,0:T(8,128)S(1)}, f32[16,1024]{1,0:T(8,128)}, u32[]{:S(2)}, u32[]{:S(2)}) collective-permute-start(f32[16,1024]{1,0:T(8,128)S(1)} %copy.16), channel_id=1, source_target_pairs={{0,32},{32,64},{64,96},{96,128},{128,160},{160,192},{192,224},{224... | collective-permute-start | bytes 196616 | tf_op jit(solution)/shard_map/while/body/eval_jaxpr/ppermute | solution.py:20
  268.5 12.3 %collective-permute-start.1 = (f32[16,1024]{1,0:T(8,128)S(1)}, f32[16,1024]{1,0:T(8,128)}, u32[]{:S(2)}, u32[]{:S(2)}) collective-permute-start(f32[16,1024]{1,0:T(8,128)S(1)} %add.226), channel_id=1, source_target_pairs={{0,32},{32,64},{64,96},{96,128},{128,160},{160,192},{192,224},{224... | collective-permute-start | bytes 196616 | tf_op jit(solution)/shard_map/while/body/eval_jaxpr/ppermute | solution.py:20
  281.7 12.8 %collective-permute-start = (f32[16,1024]{1,0:T(8,128)S(1)}, f32[16,1024]{1,0:T(8,128)}, u32[]{:S(2)}, u32[]{:S(2)}) collective-permute-start(f32[16,1024]{1,0:T(8,128)S(1)} %copy.16), channel_id=1, source_target_pairs={{0,32},{32,64},{64,96},{96,128},{128,160},{160,192},{192,224},{224... | collective-permute-start | bytes 196616 | tf_op jit(solution)/shard_map/while/body/eval_jaxpr/ppermute | solution.py:20
  287.8 12.8 %collective-permute-start.1 = (f32[16,1024]{1,0:T(8,128)S(1)}, f32[16,1024]{1,0:T(8,128)}, u32[]{:S(2)}, u32[]{:S(2)}) collective-permute-start(f32[16,1024]{1,0:T(8,128)S(1)} %add.226), channel_id=1, source_target_pairs={{0,32},{32,64},{64,96},{96,128},{128,160},{160,192},{192,224},{224... | collective-permute-start | bytes 196616 | tf_op jit(solution)/shard_map/while/body/eval_jaxpr/ppermute | solution.py:20
  301.4 12.3 %collective-permute-start = (f32[16,1024]{1,0:T(8,128)S(1)}, f32[16,1024]{1,0:T(8,128)}, u32[]{:S(2)}, u32[]{:S(2)}) collective-permute-start(f32[16,1024]{1,0:T(8,128)S(1)} %copy.16), channel_id=1, source_target_pairs={{0,32},{32,64},{64,96},{96,128},{128,160},{160,192},{192,224},{224... | collective-permute-start | bytes 196616 | tf_op jit(solution)/shard_map/while/body/eval_jaxpr/ppermute | solution.py:20
  307.5 12.3 %collective-permute-start.1 = (f32[16,1024]{1,0:T(8,128)S(1)}, f32[16,1024]{1,0:T(8,128)}, u32[]{:S(2)}, u32[]{:S(2)}) collective-permute-start(f32[16,1024]{1,0:T(8,128)S(1)} %add.226), channel_id=1, source_target_pairs={{0,32},{32,64},{64,96},{96,128},{128,160},{160,192},{192,224},{224... | collective-permute-start | bytes 196616 | tf_op jit(solution)/shard_map/while/body/eval_jaxpr/ppermute | solution.py:20
  320.7 12.3 %collective-permute-start = (f32[16,1024]{1,0:T(8,128)S(1)}, f32[16,1024]{1,0:T(8,128)}, u32[]{:S(2)}, u32[]{:S(2)}) collective-permute-start(f32[16,1024]{1,0:T(8,128)S(1)} %copy.16), channel_id=1, source_target_pairs={{0,32},{32,64},{64,96},{96,128},{128,160},{160,192},{192,224},{224... | collective-permute-start | bytes 196616 | tf_op jit(solution)/shard_map/while/body/eval_jaxpr/ppermute | solution.py:20
  326.8 12.4 %collective-permute-start.1 = (f32[16,1024]{1,0:T(8,128)S(1)}, f32[16,1024]{1,0:T(8,128)}, u32[]{:S(2)}, u32[]{:S(2)}) collective-permute-start(f32[16,1024]{1,0:T(8,128)S(1)} %add.226), channel_id=1, source_target_pairs={{0,32},{32,64},{64,96},{96,128},{128,160},{160,192},{192,224},{224... | collective-permute-start | bytes 196616 | tf_op jit(solution)/shard_map/while/body/eval_jaxpr/ppermute | solution.py:20
  (38 other events, 463.4 us)
Sparse Core Ops, SparseCore 0:
  339.3 54.8 all-gather.2
